TPU v7x, 32 devices: a whole 2x2x4 slice. The times are simulated.
32 devices in a mesh: member: 2 (over y), node: 4 (over z), feat: 4 (over x, core).
Axes of the slice: x: 2, y: 2, z: 4, core: 2. Of those that a mesh axis runs over, the one named last changes fastest.
Arguments:
- features: bfloat16 [32768, 1024], P(('member', 'node'), 'feat'), parts along dimension 0, may hold values from -6 to 6
- w_self: bfloat16 [2048, 1024], P(('member', 'node')), parts along dimension 0, may hold values from -0.125 to 0.125
- w_neigh: bfloat16 [2048, 1024], P(('member', 'node')), parts along dimension 0, may hold values from -0.125 to 0.125
- bias: float32 [2048], P('member'), parts along dimension 0, may hold values from -3 to 3
- dst_ids: int32 [4096], P('node'), may hold values from 0 to 4095, as said below
- send_blocks: int32 [4, 4, 2], P('node'), may hold values from 0 to 31, as said below
- tile_info: int32 [4, 3, 64], P('node'), may hold values from 0 to 256, as said below
- tile_edges: int32 [4, 64, 256], P('node'), may hold values from 0 to 16383, as said below
- tile_counts: int32 [4], P('node'), may hold values from 48 to 64, as said below
- cotangent: bfloat16 [8192, 1024], P(('member', 'node', 'feat')), parts along dimension 0, may hold values from -6 to 6
Outputs:
- layer_out: bfloat16 [8192, 1024], P(('member', 'node', 'feat')), parts along dimension 0
- grad_features: bfloat16 [32768, 1024], P(('member', 'node'), 'feat'), parts along dimension 0
There are 2 independent parts, one for each index of `member`. A program takes and returns all parts, laid end to end along the dimension named above; an argument that names none is the same for every part. Nothing has to cross between parts.
Inputs may be any that keep to these rules, and one draw needn't show every extreme that they name: `dst_ids`: entries 1024 * m to 1024 * (m + 1) - 1 belong to node shard m and are distinct rows of it. send_blocks[p, m, s] is a block of shard p; the 2 entries of one pair (p, m) are distinct. tile_info[m, 0, t] is a slot below 8, tile_info[m, 1, t] a destination block below 8, tile_info[m, 2, t] an edge count from 1 to 256; every shard has a tile with 256 edges. `tile_edges`: only the first tile_info[m, 2, t] entries of a tile count; in every destination block some rows receive no edge from any tile. `tile_counts`: some shard uses all 64 tiles.
All inputs are finite; a program needn't handle non-finite values.
Results may differ from a plain program's by a relative error of at most 0.0054.
Values may be sent and summed in bfloat16 or wider, within the bound.
A program may use at most 64 MiB of HBM per device.

v0:
```python
import math

import jax
import jax.numpy as jnp
from jax import lax
from jax.sharding import PartitionSpec as P

TB = 128


def activate(pre_act, cot_rows):
    sig_gate = jax.nn.sigmoid(pre_act)
    layer_out = (pre_act * sig_gate).astype(jnp.bfloat16)
    grad_pre = (
        cot_rows.astype(jnp.float32) * sig_gate * (1.0 + pre_act * (1.0 - sig_gate))
    ).astype(jnp.bfloat16)
    return (layer_out, grad_pre)


def times_rows(left, right):
    return lax.dot_general(
        left, right, (((1,), (1,)), ((), ())), preferred_element_type=jnp.float32
    )


def on_device(
    features,
    w_self,
    w_neigh,
    bias,
    dst_ids,
    send_blocks,
    tile_info,
    tile_edges,
    tile_counts,
    cotangent,
):
    node_count = lax.axis_size("node")
    row_count, col_width = features.shape
    dest_rows = dst_ids.shape[0]
    dest_blocks = dest_rows // TB
    full_self, full_neigh = (
        lax.all_gather(w_self, "node", axis=0, tiled=True),
        lax.all_gather(w_neigh, "node", axis=0, tiled=True),
    )
    local_blocks = features.reshape(row_count // TB, TB, col_width)
    chosen = send_blocks[0]
    outgoing = local_blocks[chosen]
    incoming = lax.all_to_all(outgoing, "node", split_axis=0, concat_axis=0, tiled=True)
    slot_rows = incoming.reshape(-1, TB, col_width)
    slot_total = slot_rows.shape[0]
    tile_table = tile_info[0]
    edge_codes = tile_edges[0]
    live_tiles = tile_counts[0]
    capacity, edge_slots = edge_codes.shape
    group_size = math.gcd(capacity, 16)
    turn_count = (live_tiles + group_size - 1) // group_size
    lane_ids = jnp.arange(TB)
    block_ids = jnp.arange(dest_blocks)

    def forward_step(turn_index, carry):
        aggregate, degree, stored = carry
        first_tile = turn_index * group_size
        group_codes = lax.dynamic_slice_in_dim(edge_codes, first_tile, group_size, 0)
        group_table = lax.dynamic_slice_in_dim(tile_table, first_tile, group_size, 1)
        tile_ids = first_tile + jnp.arange(group_size)
        valid_edge = (jnp.arange(edge_slots)[None, :] < group_table[2][:, None]) & (
            tile_ids < live_tiles
        )[:, None]
        source_hot = ((group_codes // TB)[:, :, None] == lane_ids).astype(jnp.bfloat16)
        target_hot = (((group_codes % TB)[:, :, None] == lane_ids) & valid_edge[:, :, None]).astype(
            jnp.bfloat16
        )
        adjacency = jnp.einsum(
            "ged,ges->gds", target_hot, source_hot, preferred_element_type=jnp.float32
        )
        adjacency_low = adjacency.astype(jnp.bfloat16)
        source_rows = slot_rows[group_table[0]]
        products = jnp.einsum(
            "gds,gsf->gdf", adjacency_low, source_rows, preferred_element_type=jnp.float32
        )
        block_hot = (group_table[1][:, None] == block_ids[None, :]).astype(jnp.float32)
        aggregate = aggregate + jnp.einsum(
            "gb,gdf->bdf", block_hot, products, precision=lax.Precision.HIGHEST
        )
        degree = degree + jnp.einsum(
            "gb,gd->bd", block_hot, jnp.sum(adjacency, axis=2), precision=lax.Precision.HIGHEST
        )
        stored = lax.dynamic_update_slice_in_dim(stored, adjacency_low, first_tile, 0)
        return (aggregate, degree, stored)

    start_carry = (
        jnp.zeros((dest_blocks, TB, col_width), jnp.float32),
        jnp.zeros((dest_blocks, TB), jnp.float32),
        jnp.zeros((capacity, TB, TB), jnp.bfloat16),
    )
    aggregate, degree, stored = lax.fori_loop(0, turn_count, forward_step, start_carry)
    row_scale = jnp.maximum(degree, 1.0)
    mean_rows = (
        (aggregate / row_scale[:, :, None]).astype(jnp.bfloat16).reshape(dest_rows, col_width)
    )
    own_rows = features[dst_ids]
    offset = lax.axis_index("feat") * col_width
    part_self = lax.dynamic_slice_in_dim(full_self, offset, col_width, 0)
    part_neigh = lax.dynamic_slice_in_dim(full_neigh, offset, col_width, 0)
    pre_act = (
        lax.psum_scatter(
            jnp.dot(own_rows, part_self, preferred_element_type=jnp.float32)
            + jnp.dot(mean_rows, part_neigh, preferred_element_type=jnp.float32),
            "feat",
            scatter_dimension=0,
            tiled=True,
        )
        + bias
    )
    layer_out, grad_pre = activate(pre_act, cotangent)
    piece_rows = lax.all_gather(grad_pre, "feat", axis=0, tiled=True)
    own_back = times_rows(piece_rows, part_self).astype(jnp.bfloat16)
    mean_back = times_rows(piece_rows, part_neigh).astype(jnp.bfloat16)
    joined = jnp.concatenate([own_back, mean_back], axis=1)
    grad_own = joined[:, :col_width]
    grad_agg = joined[:, col_width:]
    grad_sum = (
        grad_agg.astype(jnp.float32).reshape(dest_blocks, TB, col_width) / row_scale[:, :, None]
    ).astype(jnp.bfloat16)

    def backward_step(turn_index, slot_grads):
        first_tile = turn_index * group_size
        adjacency_low = lax.dynamic_slice_in_dim(stored, first_tile, group_size, 0)
        group_table = lax.dynamic_slice_in_dim(tile_table, first_tile, group_size, 1)
        target_rows = grad_sum[group_table[1]]
        products = jnp.einsum(
            "gds,gdf->gsf", adjacency_low, target_rows, preferred_element_type=jnp.float32
        )
        return slot_grads.at[group_table[0]].add(products)

    slot_grads = lax.fori_loop(
        0, turn_count, backward_step, jnp.zeros((slot_total, TB, col_width), jnp.float32)
    )
    returned = lax.all_to_all(
        slot_grads.astype(jnp.bfloat16).reshape(node_count, -1, TB, col_width),
        "node",
        split_axis=0,
        concat_axis=0,
        tiled=True,
    )
    grad_rows = jnp.zeros((row_count // TB, TB, col_width), jnp.float32)
    grad_rows = grad_rows.at[chosen.reshape(-1)].add(
        returned.reshape(-1, TB, col_width).astype(jnp.float32)
    )
    grad_rows = (
        grad_rows.reshape(row_count, col_width).at[dst_ids].add(grad_own.astype(jnp.float32))
    )
    return (layer_out, grad_rows.astype(jnp.bfloat16))


def solution(mesh):
    return jax.shard_map(
        on_device,
        mesh=mesh,
        in_specs=(
            P(("member", "node"), "feat"),
            P(("member", "node"), None),
            P(("member", "node"), None),
            P("member"),
            P("node"),
            P("node", None, None),
            P("node", None, None),
            P("node", None, None),
            P("node"),
            P(("member", "node", "feat"), None),
        ),
        out_specs=(P(("member", "node", "feat"), None), P(("member", "node"), "feat")),
        check_vma=False,
    )
```

profile of v0, /device:TPU:1, one launch (start us, length us, event | category | flops | bytes accessed | tf_op | source)
XLA Modules:
  0.0 273.6 jit_solution(16417660957997950509)
XLA Ops:
  10.2 5.4 %all-to-all-start = ((bf16[4,2,128,256]{3,2,1,0:T(8,128)(2,1)}), bf16[4,2,128,256]{3,2,1,0:T(8,128)(2,1)S(1)}, u32[]{:S(2)}, u32[]{:S(2)}) async-start(bf16[4,2,128,256]{3,2,1,0:T(8,128)(2,1)} %bitcast.8), calls=%async_computation | async-start | bytes 1048576 | tf_op jit(solution)/shard_map/all_to_all | solution.py:49
  17.1 5.0 %gather_fusion.2 = bf16[1024,256]{1,0:T(8,128)(2,1)} fusion(bf16[4096,256]{1,0:T(8,128)(2,1)S(1)} %copy-done, s32[1024]{0:T(1024)S(1)} %get-tuple-element.289), kind=kCustom, calls=%fused_computation.2 | custom fusion | bytes 1052672 | tf_op jit(solution)/shard_map/gather | solution.py:102
  22.1 14.4 %all-to-all-done = bf16[4,2,128,256]{3,2,1,0:T(8,128)(2,1)S(1)} async-done(((bf16[4,2,128,256]{3,2,1,0:T(8,128)(2,1)}), bf16[4,2,128,256]{3,2,1,0:T(8,128)(2,1)S(1)}, u32[]{:S(2)}, u32[]{:S(2)}) %all-to-all-start) | async-done | bytes 524320 | tf_op jit(solution)/shard_map/all_to_all | solution.py:49
  39.4 51.8 %while.29 = (s32[]{:T(128)}, f32[8,128,256]{2,0,1:T(8,128)}, f32[8,128]{1,0:T(8,128)S(1)}, bf16[64,128,128]{1,2,0:T(8,128)(2,1)}, s32[]{:T(128)}, /*index=5*/s32...) while((s32[]{:T(128)}, f32[8,128,256]{2,0,1:T(8,128)}, ...), condition=%wide.region_2.3_spmd.clone.clone, body=%wide.region_0.2_spmd.clone.clone.sunk | while | flops 321433920 | bytes 26359216 | solution.py:97
  40.3 5.1 %fusion.77 = (f32[16,128]{1,0:T(8,128)S(1)}, bf16[16,128,128]{1,2,0:T(8,128)(2,1)}) fusion(s32[16,256]{1,0:T(8,128)S(1)} %add_select_fusion.5, s32[16,256]{1,0:T(8,128)S(1)} %get-tuple-element.397, pred[16,256]{1,0:T(8,128)(4,1)S(1)} %fusion.76), kind=kOutput, calls=%fused_computation.83.clone.1 | convolution fusion | flops 136312832 | bytes 569344 | tf_op jit(solution)/shard_map/while/body/ged,ges->gds/dot_general | solution.py:74
  53.2 5.1 %fusion.77 = (f32[16,128]{1,0:T(8,128)S(1)}, bf16[16,128,128]{1,2,0:T(8,128)(2,1)}) fusion(s32[16,256]{1,0:T(8,128)S(1)} %add_select_fusion.5, s32[16,256]{1,0:T(8,128)S(1)} %get-tuple-element.397, pred[16,256]{1,0:T(8,128)(4,1)S(1)} %fusion.76), kind=kOutput, calls=%fused_computation.83.clone.1 | convolution fusion | flops 136312832 | bytes 569344 | tf_op jit(solution)/shard_map/while/body/ged,ges->gds/dot_general | solution.py:74
  66.1 5.1 %fusion.77 = (f32[16,128]{1,0:T(8,128)S(1)}, bf16[16,128,128]{1,2,0:T(8,128)(2,1)}) fusion(s32[16,256]{1,0:T(8,128)S(1)} %add_select_fusion.5, s32[16,256]{1,0:T(8,128)S(1)} %get-tuple-element.397, pred[16,256]{1,0:T(8,128)(4,1)S(1)} %fusion.76), kind=kOutput, calls=%fused_computation.83.clone.1 | convolution fusion | flops 136312832 | bytes 569344 | tf_op jit(solution)/shard_map/while/body/ged,ges->gds/dot_general | solution.py:74
  79.1 5.1 %fusion.77 = (f32[16,128]{1,0:T(8,128)S(1)}, bf16[16,128,128]{1,2,0:T(8,128)(2,1)}) fusion(s32[16,256]{1,0:T(8,128)S(1)} %add_select_fusion.5, s32[16,256]{1,0:T(8,128)S(1)} %get-tuple-element.397, pred[16,256]{1,0:T(8,128)(4,1)S(1)} %fusion.76), kind=kOutput, calls=%fused_computation.83.clone.1 | convolution fusion | flops 136312832 | bytes 569344 | tf_op jit(solution)/shard_map/while/body/ged,ges->gds/dot_general | solution.py:74
  92.9 3.7 %fusion.36 = f32[1024,1024]{1,0:T(8,128)} fusion(bf16[1024,256]{1,0:T(8,128)(2,1)S(1)} %copy-done.6, bf16[1024,1024]{1,0:T(8,128)(2,1)} %all-gather.4.cloned.1.call-done, s32[]{:T(128)S(6)} %select_n.99), kind=kOutput, calls=%fused_computation.69 | convolution fusion | flops 536870912 | bytes 5242884 | tf_op jit(solution)/shard_map/dot_general | solution.py:108
  96.6 14.8 %all-gather.6.cloned.1.call-done = bf16[1024,1024]{1,0:T(8,128)(2,1)} async-done(((bf16[256,1024]{1,0:T(8,128)(2,1)}), bf16[1024,1024]{1,0:T(8,128)(2,1)}) %all-gather.6.cloned.1.call-update) | async-done | bytes 2097168 | tf_op jit(solution)/shard_map/all_gather | solution.py:44
  111.3 5.0 %convolution_add_fusion.1 = f32[1024,1024]{1,0:T(8,128)} fusion(f32[1024,1024]{1,0:T(8,128)} %fusion.36, bf16[1024,256]{1,0:T(8,128)(2,1)S(1)} %bitcast.73, bf16[1024,1024]{1,0:T(8,128)(2,1)} %all-gather.6.cloned.1.call-done, s32[]{:T(128)S(6)} %select_n.99), kind=kOutput, calls=%fused_computation.54 | convolution fusion | flops 537919488 | bytes 9437188 | tf_op jit(solution)/shard_map/dot_general | solution.py:109
  116.4 43.3 %reduce-scatter.2.cloned.1.call-done = f32[256,1024]{1,0:T(8,128)} async-done(((f32[1024,1024]{1,0:T(8,128)}), f32[256,1024]{1,0:T(8,128)}) %reduce-scatter.2.cloned.1.call-update) | async-done | bytes 1048592 | tf_op jit(solution)/shard_map/reduce_scatter | solution.py:107
  159.7 2.7 multiply_convert_fusion
  162.5 23.2 %all-gather.8.cloned.1.call-done = bf16[1024,1024]{1,0:T(8,128)(2,1)} async-done(((bf16[256,1024]{1,0:T(8,128)(2,1)}), bf16[1024,1024]{1,0:T(8,128)(2,1)}) %all-gather.8.cloned.1.call-update) | async-done | bytes 2097168 | tf_op jit(solution)/shard_map/all_gather | solution.py:117
  189.1 37.4 %while.28 = (s32[]{:T(128)}, f32[8,128,256]{2,1,0:T(8,128)S(1)}, s32[]{:T(128)}, s32[3,64]{1,0:T(4,128)S(1)}, bf16[64,128,128]{1,2,0:T(8,128)(2,1)}, /*index=5*/...) while((s32[]{:T(128)}, f32[8,128,256]{2,1,0:T(8,128)S(1)}, s32[]{:T(128)}, ...), condition=%wide.region_6.7_spmd, body=%wide.region_4.6_spmd.sunk | while | flops 134743136 | bytes 12063707 | solution.py:137
  189.3 2.6 gather_fusion
  191.9 3.1 %fusion.69 = f32[16,128,256]{2,1,0:T(8,128)} fusion(bf16[16,128,256]{2,1,0:T(8,128)(2,1)} %gather_fusion, bf16[64,128,128]{1,2,0:T(8,128)(2,1)} %get-tuple-element.465, s32[]{:T(128)S(6)} %select_n.136), kind=kOutput, calls=%fused_computation.9.clone.1 | convolution fusion | flops 134217728 | bytes 3670020 | tf_op jit(solution)/shard_map/while/body/gds,gdf->gsf/dot_general | solution.py:132
  195.0 3.5 %scatter_fusion = f32[8,128,256]{2,1,0:T(8,128)S(1)} fusion(f32[8,128,256]{2,1,0:T(8,128)S(1)} %get-tuple-element.452, s32[16]{0:T(128)S(1)} %get-tuple-element.385, f32[16,128,256]{2,1,0:T(8,128)} %fusion.69), kind=kCustom, calls=%fused_computation.4.clone.1 | custom fusion | flops 524288 | bytes 6291520 | tf_op jit(solution)/shard_map/while/body/scatter-add | solution.py:135
  198.6 2.6 gather_fusion
  201.2 3.1 %fusion.69 = f32[16,128,256]{2,1,0:T(8,128)} fusion(bf16[16,128,256]{2,1,0:T(8,128)(2,1)} %gather_fusion, bf16[64,128,128]{1,2,0:T(8,128)(2,1)} %get-tuple-element.465, s32[]{:T(128)S(6)} %select_n.136), kind=kOutput, calls=%fused_computation.9.clone.1 | convolution fusion | flops 134217728 | bytes 3670020 | tf_op jit(solution)/shard_map/while/body/gds,gdf->gsf/dot_general | solution.py:132
  204.3 3.5 %scatter_fusion = f32[8,128,256]{2,1,0:T(8,128)S(1)} fusion(f32[8,128,256]{2,1,0:T(8,128)S(1)} %get-tuple-element.452, s32[16]{0:T(128)S(1)} %get-tuple-element.385, f32[16,128,256]{2,1,0:T(8,128)} %fusion.69), kind=kCustom, calls=%fused_computation.4.clone.1 | custom fusion | flops 524288 | bytes 6291520 | tf_op jit(solution)/shard_map/while/body/scatter-add | solution.py:135
  208.0 2.6 gather_fusion
  210.6 3.1 %fusion.69 = f32[16,128,256]{2,1,0:T(8,128)} fusion(bf16[16,128,256]{2,1,0:T(8,128)(2,1)} %gather_fusion, bf16[64,128,128]{1,2,0:T(8,128)(2,1)} %get-tuple-element.465, s32[]{:T(128)S(6)} %select_n.136), kind=kOutput, calls=%fused_computation.9.clone.1 | convolution fusion | flops 134217728 | bytes 3670020 | tf_op jit(solution)/shard_map/while/body/gds,gdf->gsf/dot_general | solution.py:132
  213.7 3.5 %scatter_fusion = f32[8,128,256]{2,1,0:T(8,128)S(1)} fusion(f32[8,128,256]{2,1,0:T(8,128)S(1)} %get-tuple-element.452, s32[16]{0:T(128)S(1)} %get-tuple-element.385, f32[16,128,256]{2,1,0:T(8,128)} %fusion.69), kind=kCustom, calls=%fused_computation.4.clone.1 | custom fusion | flops 524288 | bytes 6291520 | tf_op jit(solution)/shard_map/while/body/scatter-add | solution.py:135
  220.0 3.1 %fusion.69 = f32[16,128,256]{2,1,0:T(8,128)} fusion(bf16[16,128,256]{2,1,0:T(8,128)(2,1)} %gather_fusion, bf16[64,128,128]{1,2,0:T(8,128)(2,1)} %get-tuple-element.465, s32[]{:T(128)S(6)} %select_n.136), kind=kOutput, calls=%fused_computation.9.clone.1 | convolution fusion | flops 134217728 | bytes 3670020 | tf_op jit(solution)/shard_map/while/body/gds,gdf->gsf/dot_general | solution.py:132
  223.1 3.5 %scatter_fusion = f32[8,128,256]{2,1,0:T(8,128)S(1)} fusion(f32[8,128,256]{2,1,0:T(8,128)S(1)} %get-tuple-element.452, s32[16]{0:T(128)S(1)} %get-tuple-element.385, f32[16,128,256]{2,1,0:T(8,128)} %fusion.69), kind=kCustom, calls=%fused_computation.4.clone.1 | custom fusion | flops 524288 | bytes 6291520 | tf_op jit(solution)/shard_map/while/body/scatter-add | solution.py:135
  227.4 4.3 %all-to-all-start.1 = ((bf16[4,2,128,256]{3,2,1,0:T(8,128)(2,1)}), bf16[4,2,128,256]{3,2,1,0:T(8,128)(2,1)}, u32[]{:S(2)}, u32[]{:S(2)}) async-start(bf16[4,2,128,256]{3,2,1,0:T(8,128)(2,1)} %bitcast.74), calls=%async_computation.2 | async-start | bytes 1048576 | tf_op jit(solution)/shard_map/all_to_all | solution.py:140
  232.0 3.4 %fusion.30 = f32[1024,256]{1,0:T(8,128)} fusion(bf16[1024,1024]{1,0:T(8,128)(2,1)} %all-gather.8.cloned.1.call-done, bf16[1024,1024]{1,0:T(8,128)(2,1)} %all-gather.4.cloned.1.call-done, s32[]{:T(128)S(6)} %select_n.99), kind=kOutput, calls=%fused_computation.57 | convolution fusion | flops 537395200 | bytes 3670020 | tf_op jit(solution)/shard_map/dot_general | solution.py:21
  235.4 10.6 %all-to-all-done.1 = bf16[4,2,128,256]{3,2,1,0:T(8,128)(2,1)} async-done(((bf16[4,2,128,256]{3,2,1,0:T(8,128)(2,1)}), bf16[4,2,128,256]{3,2,1,0:T(8,128)(2,1)}, u32[]{:S(2)}, u32[]{:S(2)}) %all-to-all-start.1) | async-done | bytes 524320 | tf_op jit(solution)/shard_map/all_to_all | solution.py:140
  249.5 3.3 %scatter_fusion.1 = f32[32,128,256]{2,1,0:T(8,128)} fusion(f32[32,128,256]{2,1,0:T(8,128)} %broadcast_in_dim.11, s32[8]{0:T(128)S(1)} %fusion.38, f32[8,128,256]{2,1,0:T(8,128)S(1)} %bitcast_convert_fusion), kind=kCustom, calls=%fused_computation.5 | custom fusion | flops 262144 | bytes 3145760 | tf_op jit(solution)/shard_map/scatter-add | solution.py:148
  252.8 10.6 %scatter_fusion.2 = f32[4096,256]{1,0:T(8,128)} fusion(f32[4096,256]{1,0:T(8,128)} %bitcast.71, s32[1024]{0:T(1024)S(1)} %get-tuple-element.288, f32[1024,256]{1,0:T(8,128)} %fusion.30), kind=kCustom, calls=%fused_computation.6 | custom fusion | flops 262144 | bytes 3149824 | tf_op jit(solution)/shard_map/scatter-add | solution.py:152
  263.4 3.7 %convert_element_type.57 = bf16[4096,256]{1,0:T(8,128)(2,1)} convert(f32[4096,256]{1,0:T(8,128)} %scatter_fusion.2) | non-fusion elementwise | flops 1048576 | bytes 6291456 | tf_op jit(solution)/shard_map/convert_element_type | solution.py:154
  (151 shorter events, 50.5 us)
Async XLA Ops:
  7.2 1.6 copy-start
  7.2 9.9 %copy-start.12 = (s32[1,3,64]{2,0,1:T(1,128)S(1)}, s32[1,3,64]{2,0,1:T(1,128)}, u32[]{:S(2)}) copy-start(s32[1,3,64]{2,0,1:T(1,128)} %param.20) | copy-start | bytes 2308
  7.2 9.9 %copy-start.10 = (s32[1024]{0:T(1024)S(1)}, s32[1024]{0:T(1024)}, u32[]{:S(2)}) copy-start(s32[1024]{0:T(1024)} %param.18) | copy-start | bytes 12292
  7.2 85.6 %all-gather.4.cloned.1.call-start = ((), (), s32[]{:S(2)}) async-start(), calls=%async_computation.3 | async-start | bytes 2621440 | tf_op jit(solution)/shard_map/all_gather | solution.py:43
  10.2 26.3 %all-to-all-start = ((bf16[4,2,128,256]{3,2,1,0:T(8,128)(2,1)}), bf16[4,2,128,256]{3,2,1,0:T(8,128)(2,1)S(1)}, u32[]{:S(2)}, u32[]{:S(2)}) async-start(bf16[4,2,128,256]{3,2,1,0:T(8,128)(2,1)} %bitcast.8), calls=%async_computation | async-start | bytes 1048576 | tf_op jit(solution)/shard_map/all_to_all | solution.py:49
  15.6 95.7 %all-gather.6.cloned.1.call-start = ((), (), s32[]{:S(2)}) async-start(), calls=%async_computation.4 | async-start | bytes 2621440 | tf_op jit(solution)/shard_map/all_gather | solution.py:44
  16.3 143.4 %reduce-scatter.2.cloned.1.call-start = ((), (), s32[]{:S(2)}) async-start(), calls=%async_computation.5 | async-start | bytes 5242880 | tf_op jit(solution)/shard_map/reduce_scatter | solution.py:107
  22.1 17.3 %copy-start.8 = (s32[1,64,256]{2,1,0:T(8,128)S(1)}, s32[1,64,256]{2,1,0:T(8,128)}, u32[]{:S(2)}) copy-start(s32[1,64,256]{2,1,0:T(8,128)} %param.21) | copy-start | bytes 196612
  39.4 6.0 %copy-start.1 = (bf16[8,128,256]{2,1,0:T(8,128)(2,1)}, bf16[8,128,256]{2,1,0:T(8,128)(2,1)S(1)}, u32[]{:S(2)}) copy-start(bf16[8,128,256]{2,1,0:T(8,128)(2,1)S(1)} %get-tuple-element.436) | copy-start | bytes 1572868 | tf_op jit(solution)/shard_map/while
  47.2 1.6 copy-start.4
  48.8 2.3 copy-start.3
  48.8 3.5 %copy-start.2 = (bf16[8,128,256]{2,1,0:T(8,128)(2,1)S(1)}, bf16[8,128,256]{2,1,0:T(8,128)(2,1)}, u32[]{:S(2)}) copy-start(bf16[8,128,256]{2,1,0:T(8,128)(2,1)} %copy-done.1) | copy-start | bytes 1572868 | tf_op jit(solution)/shard_map/while
  52.3 6.0 %copy-start.1 = (bf16[8,128,256]{2,1,0:T(8,128)(2,1)}, bf16[8,128,256]{2,1,0:T(8,128)(2,1)S(1)}, u32[]{:S(2)}) copy-start(bf16[8,128,256]{2,1,0:T(8,128)(2,1)S(1)} %get-tuple-element.436) | copy-start | bytes 1572868 | tf_op jit(solution)/shard_map/while
  60.1 1.6 copy-start.4
  61.7 2.3 copy-start.3
  61.7 3.5 %copy-start.2 = (bf16[8,128,256]{2,1,0:T(8,128)(2,1)S(1)}, bf16[8,128,256]{2,1,0:T(8,128)(2,1)}, u32[]{:S(2)}) copy-start(bf16[8,128,256]{2,1,0:T(8,128)(2,1)} %copy-done.1) | copy-start | bytes 1572868 | tf_op jit(solution)/shard_map/while
  65.2 6.0 %copy-start.1 = (bf16[8,128,256]{2,1,0:T(8,128)(2,1)}, bf16[8,128,256]{2,1,0:T(8,128)(2,1)S(1)}, u32[]{:S(2)}) copy-start(bf16[8,128,256]{2,1,0:T(8,128)(2,1)S(1)} %get-tuple-element.436) | copy-start | bytes 1572868 | tf_op jit(solution)/shard_map/while
  73.1 1.7 copy-start.4
  74.7 2.3 copy-start.3
  74.7 3.5 %copy-start.2 = (bf16[8,128,256]{2,1,0:T(8,128)(2,1)S(1)}, bf16[8,128,256]{2,1,0:T(8,128)(2,1)}, u32[]{:S(2)}) copy-start(bf16[8,128,256]{2,1,0:T(8,128)(2,1)} %copy-done.1) | copy-start | bytes 1572868 | tf_op jit(solution)/shard_map/while
  77.0 1.2 copy-start.5
  78.2 6.0 %copy-start.1 = (bf16[8,128,256]{2,1,0:T(8,128)(2,1)}, bf16[8,128,256]{2,1,0:T(8,128)(2,1)S(1)}, u32[]{:S(2)}) copy-start(bf16[8,128,256]{2,1,0:T(8,128)(2,1)S(1)} %get-tuple-element.436) | copy-start | bytes 1572868 | tf_op jit(solution)/shard_map/while
  86.0 1.6 copy-start.4
  87.7 2.3 copy-start.3
  87.7 3.5 %copy-start.2 = (bf16[8,128,256]{2,1,0:T(8,128)(2,1)S(1)}, bf16[8,128,256]{2,1,0:T(8,128)(2,1)}, u32[]{:S(2)}) copy-start(bf16[8,128,256]{2,1,0:T(8,128)(2,1)} %copy-done.1) | copy-start | bytes 1572868 | tf_op jit(solution)/shard_map/while
  90.0 1.2 copy-start.5
  91.2 1.7 copy-start.6
  116.3 43.4 %copy-start.7 = (bf16[256,1024]{1,0:T(8,128)(2,1)S(1)}, bf16[256,1024]{1,0:T(8,128)(2,1)}, u32[]{:S(2)}) copy-start(bf16[256,1024]{1,0:T(8,128)(2,1)} %param.23) | copy-start | bytes 1572868
  116.3 43.4 %copy-start.9 = (f32[1024]{0:T(1024)S(1)}, f32[1024]{0:T(1024)}, u32[]{:S(2)}) copy-start(f32[1024]{0:T(1024)} %param.17) | copy-start | bytes 12292
  116.4 69.3 %all-gather.8.cloned.1.call-start = ((), (), s32[]{:S(2)}) async-start(), calls=%async_computation.6 | async-start | bytes 2621440 | tf_op jit(solution)/shard_map/all_gather | solution.py:117
  226.6 5.2 %copy-start.11 = (s32[1,4,2]{1,2,0:T(2,128)S(1)}, s32[1,4,2]{1,2,0:T(2,128)}, u32[]{:S(2)}) copy-start(s32[1,4,2]{1,2,0:T(2,128)} %param.19) | copy-start | bytes 100
  227.4 18.5 %all-to-all-start.1 = ((bf16[4,2,128,256]{3,2,1,0:T(8,128)(2,1)}), bf16[4,2,128,256]{3,2,1,0:T(8,128)(2,1)}, u32[]{:S(2)}, u32[]{:S(2)}) async-start(bf16[4,2,128,256]{3,2,1,0:T(8,128)(2,1)} %bitcast.74), calls=%async_computation.2 | async-start | bytes 1048576 | tf_op jit(solution)/shard_map/all_to_all | solution.py:140
  (2 other events, 2.3 us)
Sparse Core Ops, SparseCore 0:
  9.6 55.3 all-gather.3
  66.5 44.7 all-gather.5
  116.5 43.2 reduce-scatter.1
  162.6 22.9 all-gather.7
where the time goes:
time: 276 us; the launch traced here: 274 us
  waiting for transfers between devices  108 us (39%)
  matrix products  63.5 us (23%)
  other arithmetic  42.8 us (16%)
  local copies, waits for them, and re-layouts  34.7 us (13%)
  between operations  14.6 us (5%)
  starting transfers between devices  9.86 us (4%)
    reduce_scatter x1, waiting for transfers between devices, on_device(): lax.psum_scatter(jnp.dot(own_rows, part_self, preferred_element_type=jnp....  43.3 us
    all_gather x1, waiting for transfers between devices, on_device(): piece_rows = lax.all_gather(grad_pre, 'feat', axis=0, tiled=True)  23.2 us
    dot_general x4, matrix products, forward_step(): jnp.einsum('ged,ges->gds', target_hot, source_hot, preferred_element_type...  20.4 us
    all_gather x1, waiting for transfers between devices, on_device(): lax.all_gather(w_neigh, 'node', axis=0, tiled=True)  14.8 us
    all_to_all x1, waiting for transfers between devices, on_device(): lax.all_to_all(outgoing, 'node', split_axis=0, concat_axis=0, tiled=True)  14.4 us
    scatter-add x4, other arithmetic, backward_step(): return slot_grads.at[group_table[0]].add(products)  14 us
    dot_general x4, matrix products, backward_step(): jnp.einsum('gds,gdf->gsf', adjacency_low, target_rows, preferred_element_...  12.4 us
    scatter-add x1, other arithmetic, on_device(): grad_rows.reshape(row_count, col_width).at[dst_ids]  10.6 us
  transfers between devices with their start and end apart: 6, of which 5 were waited for; matrix products, arithmetic and copies ran while one was open for 25% of the time, Pallas kernels for 0%

commit v1 on v0

v1 whole, which is shorter than its diff:
```python
import functools
import math

import jax
import jax.numpy as jnp
from jax import lax
from jax.experimental import pallas as pl
from jax.experimental.pallas import tpu as pltpu
from jax.sharding import PartitionSpec as P

TB = 128
VMEM_BYTES = 60 * 1024 * 1024
F32 = jnp.float32
BF16 = jnp.bfloat16
VMEM = pl.BlockSpec(memory_space=pltpu.VMEM)
SMEM = pl.BlockSpec(memory_space=pltpu.SMEM)
ANY = pl.BlockSpec(memory_space=pl.ANY)


def dot_nn(left, right):
    return lax.dot_general(left, right, (((1,), (0,)), ((), ())), preferred_element_type=F32)


def dot_nt(left, right):
    return lax.dot_general(left, right, (((1,), (1,)), ((), ())), preferred_element_type=F32)


def prep_kernel(
    group, counts, info, send, edges, features, adj_ref, scale_ref, out_blocks, sums, sems
):
    n_dst, n_slot = sums.shape[0], sums.shape[1]
    node_count, per_node = send.shape
    copies = []
    for peer in range(node_count):
        for s in range(per_node):
            q = peer * per_node + s
            row = pl.multiple_of(send[peer, s] * TB, TB)
            copies.append(
                pltpu.make_async_copy(
                    features.at[pl.ds(row, TB), :],
                    out_blocks.at[pl.ds(q * TB, TB), :],
                    sems.at[q],
                )
            )
    for copy in copies:
        copy.start()
    edge_slots = edges.shape[1]
    live = counts[0]

    def zero(b, _):
        sums[b] = jnp.zeros(sums.shape[1:], F32)
        return 0

    lax.fori_loop(0, n_dst, zero, 0)
    sub = lax.broadcasted_iota(jnp.int32, (TB, edge_slots), 0)
    lane = lax.broadcasted_iota(jnp.int32, (1, edge_slots), 1)

    def step(i, _):
        parts = []
        for k in range(group):
            t = i * group + k
            codes = edges[pl.ds(t, 1), :]
            total = jnp.where(t < live, info[2, t], 0)
            source = codes // TB
            target = jnp.where(lane < total, codes % TB, -1)
            t_hot = jnp.where(sub == target, 1.0, 0.0).astype(BF16)
            s_hot = jnp.where(sub == source, 1.0, 0.0).astype(BF16)
            parts.append((t, dot_nt(t_hot, s_hot)))
        for t, part in parts:
            sums[info[1, t], info[0, t]] += part
        return 0

    lax.fori_loop(0, (live + group - 1) // group, step, 0)

    def finish(b, _):
        rows = pl.ds(pl.multiple_of(b * TB, TB), TB)
        total = jnp.zeros((TB, TB), F32)
        for s in range(n_slot):
            block = sums[b, s]
            total = total + block
            adj_ref[rows, s * TB : (s + 1) * TB] = block.astype(BF16)
        degree = jnp.sum(total, axis=1, keepdims=True)
        scale_ref[rows, :] = jnp.broadcast_to(jnp.maximum(degree, 1.0), (TB, TB))
        return 0

    lax.fori_loop(0, n_dst, finish, 0)
    for copy in copies:
        copy.wait()


def main_kernel(
    cfg,
    out_blocks,
    w_self,
    w_neigh,
    bias,
    adj,
    scale,
    features,
    id_col,
    id_row,
    back_row,
    cot,
    layer_ref,
    grad_ref,
    wbuf,
    adj_t,
    recv,
    own,
    mean,
    gath,
    g_own,
    g_sum,
    slot_out,
    ret,
    total,
    sbufs,
    rbufs,
    accs,
    f_send,
    f_recv,
    w_right,
    w_left,
    w_recv,
    r_send,
    r_recv,
    g_send,
    g_recv,
    b_send,
    b_recv,
):
    N, F, C, relay, WC = cfg
    L = F.bit_length() - 1
    node = lax.axis_index("node")
    feat = lax.axis_index("feat")
    bits = [(feat // (1 << j)) % 2 for j in range(L)]
    partner = [feat + (1 - 2 * bits[j]) * (1 << j) for j in range(L)]
    rows_all, cw = own.shape
    H = bias.shape[1]
    R = rows_all // F
    RC = R // C
    per = out_blocks.shape[0] // N

    def remote(src, dst, ss, rs, axis, index):
        return pltpu.make_async_remote_copy(
            src_ref=src,
            dst_ref=dst,
            send_sem=ss,
            recv_sem=rs,
            device_id={axis: index},
            device_id_type=pl.DeviceIdType.MESH,
        )

    barrier = pltpu.get_barrier_semaphore()
    for d in range(1, N):
        pl.semaphore_signal(
            barrier, inc=1, device_id={"node": (node + d) % N}, device_id_type=pl.DeviceIdType.MESH
        )
    for j in range(L):
        pl.semaphore_signal(
            barrier, inc=1, device_id={"feat": partner[j]}, device_id_type=pl.DeviceIdType.MESH
        )
    pl.semaphore_wait(barrier, N - 1 + L)

    def node_rows(index):
        return pl.ds(pl.multiple_of(index * per, per), per)

    def exchange(src, dst, ss, rs, d):
        peer = (node + d) % N
        return remote(
            src.at[node_rows(peer), :], dst.at[node_rows(node), :], ss.at[d], rs.at[d], "node", peer
        )

    for d in range(1, N):
        exchange(out_blocks, recv, f_send, f_recv, d).start()
    recv[node_rows(node), :] = out_blocks[node_rows(node), :]

    piece = cw // WC

    def w_copy(c, sem, peer):
        part = wbuf.at[c // WC, pl.ds(pl.multiple_of((c % WC) * piece, piece), piece), :]
        return remote(part, part, sem.at[c], w_recv.at[c], "node", peer)

    go_right = (node >= feat) & (node < N - 1)
    go_left = (node <= feat) & (node > 0)
    up, down = (node + 1) % N, (node + N - 1) % N

    if relay:

        @pl.when(node == feat)
        def _():
            wbuf[0] = w_self[...]
            wbuf[1] = w_neigh[...]
    else:
        wbuf[0] = w_self[...]
        wbuf[1] = w_neigh[...]

    feat_rows = features.shape[0]
    GC = 2 * WC
    own_step = rows_all // GC
    row_lane = lax.broadcasted_iota(jnp.int32, (own_step, feat_rows), 1)

    def load(c, _):
        if relay:

            @pl.when(node != feat)
            def _():
                w_copy(c, w_right, up).wait_recv()

            @pl.when(go_right)
            def _():
                w_copy(c, w_right, up).start()

            @pl.when(go_left)
            def _():
                w_copy(c, w_left, down).start()

        rows = pl.ds(pl.multiple_of(c * own_step, own_step), own_step)
        hot = jnp.where(row_lane == id_col[rows, :], 1.0, 0.0).astype(BF16)
        own[rows, :] = dot_nn(hot, features[...]).astype(BF16)
        adj_t[:, rows] = adj[rows, :].T
        return 0

    lax.fori_loop(0, GC, load, 0)

    for d in range(1, N):
        exchange(out_blocks, recv, f_send, f_recv, d).wait_recv()

    def aggregate(i, _):
        rows = pl.ds(pl.multiple_of(i * TB, TB), TB)
        value = dot_nn(adj[rows, :], recv[...]) / scale[rows, :1]
        mean[rows, :] = value.astype(BF16)
        return 0

    lax.fori_loop(0, rows_all // TB, aggregate, 0)

    def partial(g, c):
        rows = pl.ds(pl.multiple_of(g * R + c * RC, RC), RC)
        return dot_nn(own[rows, :], wbuf[0]) + dot_nn(mean[rows, :], wbuf[1])

    def r_copy(j, i, c):
        index = sum((F >> (k + 1)) * C for k in range(j)) + i * C + c
        return remote(
            sbufs[j].at[i, c],
            rbufs[j].at[i, c],
            r_send.at[index],
            r_recv.at[index],
            "feat",
            partner[j],
        )

    for c in range(C):
        for i in range(F // 2):
            sbufs[0][i, c] = partial(2 * i + 1 - bits[0], c).astype(BF16)
            r_copy(0, i, c).start()
    for c in range(C):
        for i in range(F // 2):
            accs[0][i, c] = partial(2 * i + bits[0], c)
    for j in range(1, L):
        for c in range(C):
            for a in range(F >> (j + 1)):
                for i in (2 * a, 2 * a + 1):
                    r_copy(j - 1, i, c).wait_recv()
                i = 2 * a + 1 - bits[j]
                sbufs[j][a, c] = (accs[j - 1][i, c] + rbufs[j - 1][i, c].astype(F32)).astype(BF16)
                r_copy(j, a, c).start()
                i = 2 * a + bits[j]
                accs[j][a, c] = accs[j - 1][i, c] + rbufs[j - 1][i, c].astype(F32)

    def g_copy(j, k, c, block):
        index = (j * F + k) * C + c
        part = gath.at[block, c]
        return remote(part, part, g_send.at[index], g_recv.at[index], "feat", partner[j])

    def block_of(mask):
        index = feat
        for j in range(L):
            if mask >> j & 1:
                index = index + (1 - 2 * bits[j]) * (1 << j)
        return index

    def backward(block, c):
        rows = pl.ds(pl.multiple_of(block * R + c * RC, RC), RC)
        rows_grad = gath[block, c]
        g_own[rows, :] = dot_nt(rows_grad, wbuf[0]).astype(BF16)
        to_mean = dot_nt(rows_grad, wbuf[1]).astype(BF16).astype(F32)
        g_sum[rows, :] = (to_mean / scale[rows, :1]).astype(BF16)

    for c in range(C):
        r_copy(L - 1, 0, c).wait_recv()
        pre = accs[L - 1][0, c] + rbufs[L - 1][0, c].astype(F32) + bias[...]
        sig = jax.nn.sigmoid(pre)
        rows = pl.ds(c * RC, RC)
        layer_ref[rows, :] = (pre * sig).astype(BF16)
        gath[feat, c] = (cot[rows, :].astype(F32) * sig * (1.0 + pre * (1.0 - sig))).astype(BF16)
        for j in reversed(range(L)):
            g_copy(j, 0, c, feat).start()
    for c in range(C):
        backward(feat, c)
    for c in range(C):
        for mask in sorted(range(1, F), key=lambda m: (bin(m).count("1"), m)):
            j = (mask & -mask).bit_length() - 1
            g_copy(j, mask >> (j + 1), c, block_of(mask)).wait_recv()
            for low in range(j):
                g_copy(low, mask >> (low + 1), c, block_of(mask)).start()
            backward(block_of(mask), c)

    def slot_grad(peer):
        rows = node_rows(peer)
        slot_out[rows, :] = dot_nn(adj_t[rows, :], g_sum[...]).astype(BF16)

    for d in range(1, N):
        slot_grad((node + d) % N)
        exchange(slot_out, ret, b_send, b_recv, d).start()
    slot_grad(node)
    ret[node_rows(node), :] = slot_out[node_rows(node), :]

    dst_lane = lax.broadcasted_iota(jnp.int32, (TB, rows_all), 0)

    def scatter_own(b, _):
        rows = pl.ds(pl.multiple_of(b * TB, TB), TB)
        hot = jnp.where(dst_lane + b * TB == id_row[...], 1.0, 0.0).astype(BF16)
        total[rows, :] = dot_nn(hot, g_own[...])
        return 0

    lax.fori_loop(0, feat_rows // TB, scatter_own, 0)
    for d in range(1, N):
        exchange(slot_out, ret, b_send, b_recv, d).wait_recv()
    slot_lane = lax.broadcasted_iota(jnp.int32, (TB, ret.shape[0]), 0)

    def scatter_back(b, _):
        rows = pl.ds(pl.multiple_of(b * TB, TB), TB)
        hot = jnp.where(slot_lane + b * TB == back_row[...], 1.0, 0.0).astype(BF16)
        grad_ref[rows, :] = (total[rows, :] + dot_nn(hot, ret[...])).astype(BF16)
        return 0

    lax.fori_loop(0, feat_rows // TB, scatter_back, 0)

    for d in range(1, N):
        exchange(out_blocks, recv, f_send, f_recv, d).wait_send()
        exchange(slot_out, ret, b_send, b_recv, d).wait_send()
    for j in range(L):
        for c in range(C):
            for i in range(F >> (j + 1)):
                r_copy(j, i, c).wait_send()
            for k in range(F >> (j + 1)):
                g_copy(j, k, c, block_of(k << (j + 1))).wait_send()
    if relay:

        def drain(c, _):
            @pl.when(go_right)
            def _():
                w_copy(c, w_right, up).wait_send()

            @pl.when(go_left)
            def _():
                w_copy(c, w_left, down).wait_send()

            return 0

        lax.fori_loop(0, GC, drain, 0)


def on_device(
    features,
    w_self,
    w_neigh,
    bias,
    dst_ids,
    send_blocks,
    tile_info,
    tile_edges,
    tile_counts,
    cotangent,
):
    N = lax.axis_size("node")
    F = lax.axis_size("feat")
    L = F.bit_length() - 1
    feat_rows, cw = features.shape
    rows_all = dst_ids.shape[0]
    H = bias.shape[0]
    R = rows_all // F
    C = 2
    WC = 4
    per_node = send_blocks.shape[2]
    slots = N * per_node
    slot_rows = slots * TB
    n_dst = rows_all // TB
    chosen = send_blocks[0]
    capacity = tile_edges.shape[1]

    adj, scale, out_blocks = pl.pallas_call(
        functools.partial(prep_kernel, math.gcd(capacity, 4)),
        out_shape=(
            jax.ShapeDtypeStruct((rows_all, slot_rows), BF16),
            jax.ShapeDtypeStruct((rows_all, TB), F32),
            jax.ShapeDtypeStruct((slot_rows, cw), BF16),
        ),
        in_specs=[SMEM, SMEM, SMEM, VMEM, ANY],
        out_specs=(VMEM, VMEM, ANY),
        scratch_shapes=[
            pltpu.VMEM((n_dst, slots, TB, TB), F32),
            pltpu.SemaphoreType.DMA((slots,)),
        ],
        compiler_params=pltpu.CompilerParams(vmem_limit_bytes=VMEM_BYTES),
        name="prep",
    )(tile_counts, tile_info[0], chosen, tile_edges[0], features)

    relay = N == F and w_self.shape[0] == cw
    if not relay:
        offset = lax.axis_index("feat") * cw
        w_self, w_neigh = (
            lax.dynamic_slice_in_dim(
                lax.all_gather(w, "node", axis=0, tiled=True), offset, cw, 0
            )
            for w in (w_self, w_neigh)
        )
    back_ids = (chosen.reshape(-1, 1) * TB + jnp.arange(TB)[None, :]).reshape(1, -1)
    dma = pltpu.SemaphoreType.DMA
    halves = [F >> (j + 1) for j in range(L)]
    layer_out, grad_rows = pl.pallas_call(
        functools.partial(main_kernel, (N, F, C, relay, WC)),
        out_shape=(
            jax.ShapeDtypeStruct((R, H), BF16),
            jax.ShapeDtypeStruct((feat_rows, cw), BF16),
        ),
        in_specs=[VMEM] * 11,
        out_specs=(VMEM, VMEM),
        scratch_shapes=[
            pltpu.VMEM((2, cw, H), BF16),
            pltpu.VMEM((slot_rows, rows_all), BF16),
            pltpu.VMEM((slot_rows, cw), BF16),
            pltpu.VMEM((rows_all, cw), BF16),
            pltpu.VMEM((rows_all, cw), BF16),
            pltpu.VMEM((F, C, R // C, H), BF16),
            pltpu.VMEM((rows_all, cw), BF16),
            pltpu.VMEM((rows_all, cw), BF16),
            pltpu.VMEM((slot_rows, cw), BF16),
            pltpu.VMEM((slot_rows, cw), BF16),
            pltpu.VMEM((feat_rows, cw), F32),
            [pltpu.VMEM((h, C, R // C, H), BF16) for h in halves],
            [pltpu.VMEM((h, C, R // C, H), BF16) for h in halves],
            [pltpu.VMEM((h, C, R // C, H), F32) for h in halves],
            dma((N,)),
            dma((N,)),
            dma((2 * WC,)),
            dma((2 * WC,)),
            dma((2 * WC,)),
            dma((F * C,)),
            dma((F * C,)),
            dma((L * F * C,)),
            dma((L * F * C,)),
            dma((N,)),
            dma((N,)),
        ],
        compiler_params=pltpu.CompilerParams(
            collective_id=0, has_side_effects=True, vmem_limit_bytes=VMEM_BYTES
        ),
        name="layer",
    )(
        out_blocks,
        w_self,
        w_neigh,
        bias.reshape(1, H),
        adj,
        scale,
        features,
        dst_ids.reshape(-1, 1),
        dst_ids.reshape(1, -1),
        back_ids,
        cotangent,
    )
    return (layer_out, grad_rows)


def solution(mesh):
    return jax.shard_map(
        on_device,
        mesh=mesh,
        in_specs=(
            P(("member", "node"), "feat"),
            P(("member", "node"), None),
            P(("member", "node"), None),
            P("member"),
            P("node"),
            P("node", None, None),
            P("node", None, None),
            P("node", None, None),
            P("node"),
            P(("member", "node", "feat"), None),
        ),
        out_specs=(P(("member", "node", "feat"), None), P(("member", "node"), "feat")),
        check_vma=False,
    )
```

time: 276 us -> 129 us (0.47)
  Pallas kernels: 0 us -> 117 us
  waiting for transfers between devices: 108 us -> 0 us
  matrix products: 63.5 us -> 0 us
  other arithmetic: 42.8 us -> 1.35 us
  local copies, waits for them, and re-layouts: 34.7 us -> 9.43 us
  between operations: 14.6 us -> 1.3 us
  starting transfers between devices: 9.86 us -> 0 us
    pallas_call x0 -> x2, Pallas kernels: none -> 117 us  [the longest x1 97.6 us: on_device(): pl.pallas_call(functools.partial(main_kernel, (N, F, C, relay, WC)), out_...]
    dot_general x24 -> x0, matrix products: 63.5 us -> none  [the longest x4 20.4 us: forward_step(): jnp.einsum('ged,ges->gds', target_hot, source_hot, preferred_element_type...]
    reduce_scatter x1 -> x0, waiting for transfers between devices: 43.3 us -> none  [on_device(): lax.psum_scatter(jnp.dot(own_rows, part_self, preferred_element_type=jnp....]
    all_gather x3 -> x0, waiting for transfers between devices: 38 us -> none  [the longest x1 23.2 us: on_device(): piece_rows = lax.all_gather(grad_pre, 'feat', axis=0, tiled=True)]
    scatter-add x6 -> x0, other arithmetic: 27.9 us -> none  [the longest x4 14 us: backward_step(): return slot_grads.at[group_table[0]].add(products)]
    all_to_all x2 -> x0, waiting for transfers between devices: 24.9 us -> none  [the longest x1 14.4 us: on_device(): lax.all_to_all(outgoing, 'node', split_axis=0, concat_axis=0, tiled=True)]
    gather x10 -> x0, local copies, waits for them, and re-layouts: 23.6 us -> none  [the longest x4 10.5 us: backward_step(): target_rows = grad_sum[group_table[1]]]
    convert_element_type x6 -> x0, other arithmetic: 11 us -> none  [the longest x1 3.71 us: on_device(): return (layer_out, grad_rows.astype(jnp.bfloat16))]
  transfers between devices with their start and end apart: 6 -> 0, of which waited for: 5 -> 0; matrix products, arithmetic and copies ran while one was open for 25% -> 0% of each run, Pallas kernels for 0% -> 0%
where the time goes in v1:
time: 129 us
  Pallas kernels  117 us (91%)
  local copies, waits for them, and re-layouts  9.43 us (7%)
  other arithmetic  1.35 us (1%)
  between operations  1.3 us (1%)
    pallas_call x1, Pallas kernels, on_device(): pl.pallas_call(functools.partial(main_kernel, (N, F, C, relay, WC)), out_...  97.6 us
    pallas_call x1, Pallas kernels, on_device(): pl.pallas_call(functools.partial(prep_kernel, math.gcd(capacity, 4)), out...  19.4 us
    unnamed x3, local copies, waits for them, and re-layouts  6.19 us

profile of v1, /device:TPU:1, one launch (start us, length us, event | category | flops | bytes accessed | tf_op | source)
XLA Modules:
  0.0 129.1 jit_solution(2496395108795915391)
XLA Ops:
  1.3 0.7 broadcast_multiply_fusion
  2.0 0.1 copy.15
  2.1 0.1 mul.12
  2.1 1.3 copy.19
  3.4 1.3 %copy.14.send = s32[4,2]{1,0:T(4,128)} copy(s32[4,2]{0,1:T(2,128)} %bitcast.15) | data formatting | bytes 64 | tf_op jit(solution)/shard_map/squeeze | solution.py:389
  4.8 0.7 iota_add_fusion
  5.4 1.7 %copy.16.id_col = s32[1024,1]{1,0:T(8,128)} copy(s32[1024,1]{0,1:T(1,128)} %bitcast.10) | data formatting | bytes 8192 | tf_op jit(solution)/shard_map/reshape | solution.py:468
  7.1 19.4 %prep.1 = (bf16[1024,1024]{1,0:T(8,128)(2,1)}, f32[1024,128]{1,0:T(8,128)}, bf16[1024,256]{1,0:T(8,128)(2,1)}) custom-call(s32[1]{0:T(128)S(6)} %copy.22.counts, s32[3,64]{1,0:T(4,128)} %bitcast.13, s32[4,2]{1,0:T(4,128)} %copy.14.send, s32[64,256]{1,0:T(8,128)} %bitcast.9, bf16[4096,256]{1,0:T(8,128)(2,1)} %features.3), custom_call_target="tpu_custom_call" | custom-call | tf_op jit(solution)/shard_map/prep/pallas_call | solution.py:392
  26.5 97.6 %layer.1 = (bf16[256,1024]{1,0:T(8,128)(2,1)}, bf16[4096,256]{1,0:T(8,128)(2,1)}) custom-call(bf16[1024,256]{1,0:T(8,128)(2,1)} %get-tuple-element.5.out_blocks, bf16[256,1024]{1,0:T(8,128)(2,1)} %w_self.1, bf16[256,1024]{1,0:T(8,128)(2,1)} %w_neigh.1, f32[1,1024]{1,0:T(1,128)} %bitcast.14, bf16[1024,1024]{1,0:T(8,128)(2,1)} %get-tuple-element.6.adj, ...), custom_call_target="tpu_custom_call" | custom-call | tf_op jit(solution)/shard_map/layer/pallas_call | solution.py:421
  124.2 1.9 %copy.23 = bf16[256,1024]{1,0:T(8,128)(2,1)} copy(bf16[256,1024]{1,0:T(8,128)(2,1)} %get-tuple-element.10) | data formatting | bytes 1048576
  126.1 3.0 %copy.24 = bf16[4096,256]{1,0:T(8,128)(2,1)} copy(bf16[4096,256]{1,0:T(8,128)(2,1)} %get-tuple-element.11) | data formatting | bytes 4194304

commit v2 on v1

--- a/solution.py
+++ b/solution.py
@@ -25,16 +25,13 @@
     return lax.dot_general(left, right, (((1,), (1,)), ((), ())), preferred_element_type=F32)
 
 
-def prep_kernel(
-    group, counts, info, send, edges, features, adj_ref, scale_ref, out_blocks, sums, sems
-):
-    n_dst, n_slot = sums.shape[0], sums.shape[1]
-    node_count, per_node = send.shape
+def plan_kernel(n_slot, counts, send, info, edges, features, src_ref, dst_ref, bound_ref, out_blocks, sems):
+    per_node, node_count = send.shape
     copies = []
     for peer in range(node_count):
         for s in range(per_node):
             q = peer * per_node + s
-            row = pl.multiple_of(send[peer, s] * TB, TB)
+            row = pl.multiple_of(send[s, peer] * TB, TB)
             copies.append(
                 pltpu.make_async_copy(
                     features.at[pl.ds(row, TB), :],
@@ -44,48 +41,53 @@
             )
     for copy in copies:
         copy.start()
-    edge_slots = edges.shape[1]
+    capacity, edge_slots = edges.shape
     live = counts[0]
-
-    def zero(b, _):
-        sums[b] = jnp.zeros(sums.shape[1:], F32)
-        return 0
-
-    lax.fori_loop(0, n_dst, zero, 0)
-    sub = lax.broadcasted_iota(jnp.int32, (TB, edge_slots), 0)
-    lane = lax.broadcasted_iota(jnp.int32, (1, edge_slots), 1)
-
-    def step(i, _):
-        parts = []
-        for k in range(group):
-            t = i * group + k
-            codes = edges[pl.ds(t, 1), :]
-            total = jnp.where(t < live, info[2, t], 0)
-            source = codes // TB
-            target = jnp.where(lane < total, codes % TB, -1)
-            t_hot = jnp.where(sub == target, 1.0, 0.0).astype(BF16)
-            s_hot = jnp.where(sub == source, 1.0, 0.0).astype(BF16)
-            parts.append((t, dot_nt(t_hot, s_hot)))
-        for t, part in parts:
-            sums[info[1, t], info[0, t]] += part
-        return 0
-
-    lax.fori_loop(0, (live + group - 1) // group, step, 0)
-
-    def finish(b, _):
-        rows = pl.ds(pl.multiple_of(b * TB, TB), TB)
-        total = jnp.zeros((TB, TB), F32)
-        for s in range(n_slot):
-            block = sums[b, s]
-            total = total + block
-            adj_ref[rows, s * TB : (s + 1) * TB] = block.astype(BF16)
-        degree = jnp.sum(total, axis=1, keepdims=True)
-        scale_ref[rows, :] = jnp.broadcast_to(jnp.maximum(degree, 1.0), (TB, TB))
-        return 0
-
-    lax.fori_loop(0, n_dst, finish, 0)
+    width = bound_ref.shape[1]
+    tile = lax.broadcasted_iota(jnp.int32, (1, capacity), 1)
+    key = jnp.where(tile < live, info[1] * n_slot + info[0], width).astype(F32)
+    total = jnp.where(tile < live, info[2], 0).astype(F32)
+    lane = lax.broadcasted_iota(jnp.int32, (capacity, capacity), 1)
+    sub = lax.broadcasted_iota(jnp.int32, (capacity, capacity), 0)
+    diag = lane == sub
+
+    def column(row):
+        return jnp.sum(jnp.where(diag, jnp.broadcast_to(row, diag.shape), 0.0), axis=1, keepdims=True)
+
+    key_col = column(key)
+    before = (key_col < key) | ((key_col == key) & (sub < lane))
+    rank = jnp.sum(jnp.where(before, 1.0, 0.0), axis=0, keepdims=True)
+    order = jnp.where(sub.astype(F32) == rank, 1.0, 0.0).astype(BF16)
+    slot_lane = lax.broadcasted_iota(jnp.int32, (capacity, width), 1).astype(F32)
+    bound = jnp.sum(jnp.where(key_col < slot_lane, 1.0, 0.0), axis=0, keepdims=True)
+    bound_ref[...] = bound.astype(jnp.int32)
+    codes = edges[...]
+    place = lax.broadcasted_iota(jnp.int32, (capacity, edge_slots), 1).astype(F32)
+    source = (codes // TB).astype(F32)
+    target = jnp.where(place < column(total), (codes % TB).astype(F32), -1.0)
+    src_ref[...] = dot_nn(order, source.astype(BF16))
+    dst_ref[...] = dot_nn(order, target.astype(BF16))
     for copy in copies:
         copy.wait()
+
+
+def final_kernel(send, base, back, layer, grad_ref, layer_ref, rows_sum):
+    per_node, node_count = send.shape
+    step = pl.program_id(0)
+    layer_ref[...] = layer[...]
+    rows_sum[...] = base[...].astype(F32)
+    blocks = rows_sum.shape[0] // TB
+    for peer in range(node_count):
+        for s in range(per_node):
+            q = peer * per_node + s
+            local = send[s, peer] - step * blocks
+
+            @pl.when((local >= 0) & (local < blocks))
+            def _():
+                rows = pl.ds(pl.multiple_of(local * TB, TB), TB)
+                rows_sum[rows, :] += back[q * TB : (q + 1) * TB, :].astype(F32)
+
+    grad_ref[...] = rows_sum[...].astype(BF16)
 
 
 def main_kernel(
@@ -94,17 +96,20 @@
     w_self,
     w_neigh,
     bias,
-    adj,
-    scale,
+    src_of,
+    dst_of,
+    bounds,
     features,
-    id_col,
     id_row,
-    back_row,
     cot,
     layer_ref,
-    grad_ref,
+    ret,
+    base_ref,
     wbuf,
+    prefix,
+    adj,
     adj_t,
+    scale,
     recv,
     own,
     mean,
@@ -112,7 +117,6 @@
     g_own,
     g_sum,
     slot_out,
-    ret,
     total,
     sbufs,
     rbufs,
@@ -128,6 +132,7 @@
     g_recv,
     b_send,
     b_recv,
+    out_sem,
 ):
     N, F, C, relay, WC = cfg
     L = F.bit_length() - 1
@@ -198,9 +203,36 @@
     feat_rows = features.shape[0]
     GC = 2 * WC
     own_step = rows_all // GC
-    row_lane = lax.broadcasted_iota(jnp.int32, (own_step, feat_rows), 1)
+    capacity, edge_slots = src_of.shape
+    n_dst = rows_all // TB
+    n_slot = recv.shape[0] // TB
+    group = capacity // GC
+    sub_f = lax.broadcasted_iota(jnp.int32, (TB, edge_slots), 0).astype(BF16)
+    one, nil = jnp.ones((), BF16), jnp.zeros((), BF16)
+    lane_id = lax.broadcasted_iota(jnp.int32, (TB, TB), 1)
+    prefix[0] = jnp.zeros((TB, TB), F32)
 
     def load(c, _):
+        running = prefix[c * group]
+        for k in range(group):
+            t = c * group + k
+            source = jnp.broadcast_to(src_of[pl.ds(t, 1), :].astype(BF16), sub_f.shape)
+            target = jnp.broadcast_to(dst_of[pl.ds(t, 1), :].astype(BF16), sub_f.shape)
+            t_hot = jnp.where(sub_f == target, one, nil)
+            s_hot = jnp.where(sub_f == source, one, nil)
+            running = running + dot_nt(t_hot, s_hot)
+            prefix[t + 1] = running
+        for k in range(own_step // TB):
+            rows = pl.ds(pl.multiple_of(c * own_step + k * TB, TB), TB)
+            ids = jnp.broadcast_to(id_row[:, rows].astype(F32), (TB, TB)).T.astype(jnp.int32)
+            hot = jnp.concatenate(
+                [
+                    jnp.where(lane_id + b * TB == ids, 1.0, 0.0).astype(BF16)
+                    for b in range(feat_rows // TB)
+                ],
+                axis=1,
+            )
+            own[rows, :] = dot_nn(hot, features[...]).astype(BF16)
         if relay:
 
             @pl.when(node != feat)
@@ -215,13 +247,24 @@
             def _():
                 w_copy(c, w_left, down).start()
 
-        rows = pl.ds(pl.multiple_of(c * own_step, own_step), own_step)
-        hot = jnp.where(row_lane == id_col[rows, :], 1.0, 0.0).astype(BF16)
-        own[rows, :] = dot_nn(hot, features[...]).astype(BF16)
-        adj_t[:, rows] = adj[rows, :].T
         return 0
 
     lax.fori_loop(0, GC, load, 0)
+
+    def assemble(b, _):
+        rows = pl.ds(pl.multiple_of(b * TB, TB), TB)
+        degree = jnp.zeros((TB, TB), F32)
+        for s in range(n_slot):
+            low, high = bounds[0, b * n_slot + s], bounds[0, b * n_slot + s + 1]
+            block = prefix[high] - prefix[low]
+            degree = degree + block
+            adj[rows, s * TB : (s + 1) * TB] = block.astype(BF16)
+            adj_t[s * TB : (s + 1) * TB, rows] = block.T.astype(BF16)
+        degree = jnp.sum(degree, axis=1, keepdims=True)
+        scale[rows, :] = jnp.broadcast_to(jnp.maximum(degree, 1.0), (TB, TB))
+        return 0
+
+    lax.fori_loop(0, n_dst, assemble, 0)
 
     for d in range(1, N):
         exchange(out_blocks, recv, f_send, f_recv, d).wait_recv()
@@ -320,21 +363,22 @@
     def scatter_own(b, _):
         rows = pl.ds(pl.multiple_of(b * TB, TB), TB)
         hot = jnp.where(dst_lane + b * TB == id_row[...], 1.0, 0.0).astype(BF16)
-        total[rows, :] = dot_nn(hot, g_own[...])
+        total[rows, :] = dot_nn(hot, g_own[...]).astype(BF16)
         return 0
 
-    lax.fori_loop(0, feat_rows // TB, scatter_own, 0)
+    quarter = feat_rows // 4
+
+    def put(k):
+        rows = pl.ds(k * quarter, quarter)
+        return pltpu.make_async_copy(total.at[rows, :], base_ref.at[rows, :], out_sem.at[k])
+
+    for k in range(4):
+        lax.fori_loop(k * quarter // TB, (k + 1) * quarter // TB, scatter_own, 0)
+        put(k).start()
     for d in range(1, N):
         exchange(slot_out, ret, b_send, b_recv, d).wait_recv()
-    slot_lane = lax.broadcasted_iota(jnp.int32, (TB, ret.shape[0]), 0)
-
-    def scatter_back(b, _):
-        rows = pl.ds(pl.multiple_of(b * TB, TB), TB)
-        hot = jnp.where(slot_lane + b * TB == back_row[...], 1.0, 0.0).astype(BF16)
-        grad_ref[rows, :] = (total[rows, :] + dot_nn(hot, ret[...])).astype(BF16)
-        return 0
-
-    lax.fori_loop(0, feat_rows // TB, scatter_back, 0)
+    for k in range(4):
+        put(k).wait()
 
     for d in range(1, N):
         exchange(out_blocks, recv, f_send, f_recv, d).wait_send()
@@ -386,25 +430,25 @@
     slots = N * per_node
     slot_rows = slots * TB
     n_dst = rows_all // TB
-    chosen = send_blocks[0]
     capacity = tile_edges.shape[1]
 
-    adj, scale, out_blocks = pl.pallas_call(
-        functools.partial(prep_kernel, math.gcd(capacity, 4)),
+    send = jnp.swapaxes(send_blocks, 1, 2)[0]
+    info = jnp.swapaxes(tile_info, 0, 1)
+    width = -(-(n_dst * slots + 1) // TB) * TB
+    src_of, dst_of, bounds, out_blocks = pl.pallas_call(
+        functools.partial(plan_kernel, slots),
         out_shape=(
-            jax.ShapeDtypeStruct((rows_all, slot_rows), BF16),
-            jax.ShapeDtypeStruct((rows_all, TB), F32),
+            jax.ShapeDtypeStruct(tile_edges.shape[1:], F32),
+            jax.ShapeDtypeStruct(tile_edges.shape[1:], F32),
+            jax.ShapeDtypeStruct((1, width), jnp.int32),
             jax.ShapeDtypeStruct((slot_rows, cw), BF16),
         ),
-        in_specs=[SMEM, SMEM, SMEM, VMEM, ANY],
-        out_specs=(VMEM, VMEM, ANY),
-        scratch_shapes=[
-            pltpu.VMEM((n_dst, slots, TB, TB), F32),
-            pltpu.SemaphoreType.DMA((slots,)),
-        ],
+        in_specs=[SMEM, SMEM, VMEM, VMEM, ANY],
+        out_specs=(VMEM, VMEM, VMEM, VMEM),
+        scratch_shapes=[pltpu.SemaphoreType.DMA((slots,))],
         compiler_params=pltpu.CompilerParams(vmem_limit_bytes=VMEM_BYTES),
-        name="prep",
-    )(tile_counts, tile_info[0], chosen, tile_edges[0], features)
+        name="plan",
+    )(tile_counts, send, info, tile_edges[0], features)
 
     relay = N == F and w_self.shape[0] == cw
     if not relay:
@@ -415,20 +459,23 @@
             )
             for w in (w_self, w_neigh)
         )
-    back_ids = (chosen.reshape(-1, 1) * TB + jnp.arange(TB)[None, :]).reshape(1, -1)
     dma = pltpu.SemaphoreType.DMA
     halves = [F >> (j + 1) for j in range(L)]
-    layer_out, grad_rows = pl.pallas_call(
+    layer_rows, back, base = pl.pallas_call(
         functools.partial(main_kernel, (N, F, C, relay, WC)),
         out_shape=(
             jax.ShapeDtypeStruct((R, H), BF16),
+            jax.ShapeDtypeStruct((slot_rows, cw), BF16),
             jax.ShapeDtypeStruct((feat_rows, cw), BF16),
         ),
-        in_specs=[VMEM] * 11,
-        out_specs=(VMEM, VMEM),
+        in_specs=[VMEM] * 6 + [SMEM] + [VMEM] * 3,
+        out_specs=(VMEM, VMEM, ANY),
         scratch_shapes=[
             pltpu.VMEM((2, cw, H), BF16),
+            pltpu.VMEM((capacity + 1, TB, TB), F32),
+            pltpu.VMEM((rows_all, slot_rows), BF16),
             pltpu.VMEM((slot_rows, rows_all), BF16),
+            pltpu.VMEM((rows_all, TB), F32),
             pltpu.VMEM((slot_rows, cw), BF16),
             pltpu.VMEM((rows_all, cw), BF16),
             pltpu.VMEM((rows_all, cw), BF16),
@@ -436,8 +483,7 @@
             pltpu.VMEM((rows_all, cw), BF16),
             pltpu.VMEM((rows_all, cw), BF16),
             pltpu.VMEM((slot_rows, cw), BF16),
-            pltpu.VMEM((slot_rows, cw), BF16),
-            pltpu.VMEM((feat_rows, cw), F32),
+            pltpu.VMEM((feat_rows, cw), BF16),
             [pltpu.VMEM((h, C, R // C, H), BF16) for h in halves],
             [pltpu.VMEM((h, C, R // C, H), BF16) for h in halves],
             [pltpu.VMEM((h, C, R // C, H), F32) for h in halves],
@@ -452,6 +498,7 @@
             dma((L * F * C,)),
             dma((N,)),
             dma((N,)),
+            dma((4,)),
         ],
         compiler_params=pltpu.CompilerParams(
             collective_id=0, has_side_effects=True, vmem_limit_bytes=VMEM_BYTES
@@ -462,14 +509,35 @@
         w_self,
         w_neigh,
         bias.reshape(1, H),
-        adj,
-        scale,
+        src_of,
+        dst_of,
+        bounds,
         features,
-        dst_ids.reshape(-1, 1),
         dst_ids.reshape(1, -1),
-        back_ids,
         cotangent,
     )
+    steps = math.gcd(math.gcd(feat_rows // TB, R // 16), 8)
+    grad_rows, layer_out = pl.pallas_call(
+        final_kernel,
+        grid=(steps,),
+        out_shape=(
+            jax.ShapeDtypeStruct((feat_rows, cw), BF16),
+            jax.ShapeDtypeStruct((R, H), BF16),
+        ),
+        in_specs=[
+            SMEM,
+            pl.BlockSpec((feat_rows // steps, cw), lambda i: (i, 0)),
+            pl.BlockSpec((slot_rows, cw), lambda i: (0, 0)),
+            pl.BlockSpec((R // steps, H), lambda i: (i, 0)),
+        ],
+        out_specs=(
+            pl.BlockSpec((feat_rows // steps, cw), lambda i: (i, 0)),
+            pl.BlockSpec((R // steps, H), lambda i: (i, 0)),
+        ),
+        scratch_shapes=[pltpu.VMEM((feat_rows // steps, cw), F32)],
+        compiler_params=pltpu.CompilerParams(vmem_limit_bytes=VMEM_BYTES),
+        name="finish",
+    )(send, base, back, layer_rows)
     return (layer_out, grad_rows)
 
 

time: 129 us -> 102 us (0.79)
  Pallas kernels: 117 us -> 99.9 us
  local copies, waits for them, and re-layouts: 9.43 us -> 0 us
  other arithmetic: 1.35 us -> 0 us
    pallas_call x1 -> x2, Pallas kernels: 19.4 us -> 9.36 us  [the longest x1 6.52 us: on_device(): pl.pallas_call(final_kernel, grid=(steps,), out_shape=(jax.ShapeDtypeStru...]
    pallas_call x1, Pallas kernels: 97.6 us -> 90.6 us  [on_device(): pl.pallas_call(functools.partial(main_kernel, (N, F, C, relay, WC)), out_...]
    unnamed x3 -> x0, local copies, waits for them, and re-layouts: 6.19 us -> none
    reshape x1 -> x0, local copies, waits for them, and re-layouts: 1.72 us -> none  [on_device(): dst_ids.reshape(-1, 1)]
    squeeze x1 -> x0, local copies, waits for them, and re-layouts: 1.35 us -> none  [on_device(): chosen = send_blocks[0]]
where the time goes in v2:
time: 102 us; the launch traced here: 101 us
  Pallas kernels  99.9 us (98%)
  between operations  1.29 us (1%)
    pallas_call x1, Pallas kernels, on_device(): pl.pallas_call(functools.partial(main_kernel, (N, F, C, relay, WC)), out_...  90.6 us
    pallas_call x1, Pallas kernels, on_device(): pl.pallas_call(final_kernel, grid=(steps,), out_shape=(jax.ShapeDtypeStru...  6.52 us
    pallas_call x1, Pallas kernels, on_device(): pl.pallas_call(functools.partial(plan_kernel, slots), out_shape=(jax.Shap...  2.84 us

profile of v2, /device:TPU:1, one launch (start us, length us, event | category | flops | bytes accessed | tf_op | source)
XLA Modules:
  0.0 101.2 jit_solution(17182293652611813434)
XLA Ops:
  1.3 2.8 %plan.1 = (f32[64,256]{1,0:T(8,128)}, f32[64,256]{1,0:T(8,128)}, s32[1,128]{1,0:T(1,128)}, bf16[1024,256]{1,0:T(8,128)(2,1)}) custom-call(s32[1]{0:T(128)S(6)} %copy.12.counts, s32[2,4]{1,0:T(2,128)} %bitcast.10, s32[3,1,64]{2,1,0:T(1,128)} %bitcast.12, s32[64,256]{1,0:T(8,128)} %bitcast.7, bf16[4096,256]{1,0:T(8,128)(2,1)} %features.3), custom_call_target="tpu_custom_call" | custom-call | tf_op jit(solution)/shard_map/plan/pallas_call | solution.py:438
  4.1 90.6 %layer.1 = (bf16[256,1024]{1,0:T(8,128)(2,1)}, bf16[1024,256]{1,0:T(8,128)(2,1)}, bf16[4096,256]{1,0:T(8,128)(2,1)}) custom-call(bf16[1024,256]{1,0:T(8,128)(2,1)} %get-tuple-element.11.out_blocks, bf16[256,1024]{1,0:T(8,128)(2,1)} %w_self.1, bf16[256,1024]{1,0:T(8,128)(2,1)} %w_neigh.1, f32[1,1024]{1,0:T(1,128)} %bitcast.8, ...), custom_call_target="tpu_custom_call" | custom-call | tf_op jit(solution)/shard_map/layer/pallas_call | solution.py:464
  94.7 6.5 %finish.1 = (bf16[4096,256]{1,0:T(8,128)(2,1)}, bf16[256,1024]{1,0:T(8,128)(2,1)}) custom-call(s32[2,4]{1,0:T(2,128)} %bitcast.11, bf16[4096,256]{1,0:T(8,128)(2,1)} %get-tuple-element.15.base, bf16[1024,256]{1,0:T(8,128)(2,1)} %get-tuple-element.16.back, bf16[256,1024]{1,0:T(8,128)(2,1)} %get-tuple-element.17.layer), custom_call_target="tpu_custom_call" | custom-call | tf_op jit(solution)/shard_map/finish/pallas_call | solution.py:520

commit v3 on v2

--- a/solution.py
+++ b/solution.py
@@ -106,6 +106,7 @@
     ret,
     base_ref,
     wbuf,
+    wvia,
     prefix,
     adj,
     adj_t,
@@ -123,9 +124,10 @@
     accs,
     f_send,
     f_recv,
-    w_right,
-    w_left,
+    w_send,
     w_recv,
+    h_send,
+    h_recv,
     r_send,
     r_recv,
     g_send,
@@ -180,15 +182,26 @@
         exchange(out_blocks, recv, f_send, f_recv, d).start()
     recv[node_rows(node), :] = out_blocks[node_rows(node), :]
 
-    piece = cw // WC
-
-    def w_copy(c, sem, peer):
-        part = wbuf.at[c // WC, pl.ds(pl.multiple_of((c % WC) * piece, piece), piece), :]
-        return remote(part, part, sem.at[c], w_recv.at[c], "node", peer)
-
-    go_right = (node >= feat) & (node < N - 1)
-    go_left = (node <= feat) & (node > 0)
+    GC = 2 * WC
+    piece = cw // GC
+    across = partner[L - 1]
     up, down = (node + 1) % N, (node + N - 1) % N
+
+    def w_rows(c):
+        return pl.ds(pl.multiple_of(c * piece, piece), piece)
+
+    def w_copy(c, way, side, peer):
+        part = (wbuf.at[0] if way == 0 else wvia).at[w_rows(c), :]
+        return remote(part, part, w_send.at[way, side, c], w_recv.at[way, c], "node", peer)
+
+    def hop_copy(c):
+        return remote(
+            wvia.at[w_rows(c), :], wbuf.at[1, w_rows(c), :], h_send.at[c], h_recv.at[c], "feat", across
+        )
+
+    roots = (feat, across)
+    go_right = [(node >= r) & (node < N - 1) for r in roots]
+    go_left = [(node <= r) & (node > 0) for r in roots]
 
     if relay:
 
@@ -196,12 +209,15 @@
         def _():
             wbuf[0] = w_self[...]
             wbuf[1] = w_neigh[...]
+
+        @pl.when(node == across)
+        def _():
+            wvia[...] = w_neigh[...]
     else:
         wbuf[0] = w_self[...]
         wbuf[1] = w_neigh[...]
 
     feat_rows = features.shape[0]
-    GC = 2 * WC
     own_step = rows_all // GC
     capacity, edge_slots = src_of.shape
     n_dst = rows_all // TB
@@ -235,17 +251,23 @@
             own[rows, :] = dot_nn(hot, features[...]).astype(BF16)
         if relay:
 
-            @pl.when(node != feat)
+            for way in range(2):
+
+                @pl.when(node != roots[way])
+                def _():
+                    w_copy(c, way, 0, up).wait_recv()
+
+                @pl.when(go_right[way])
+                def _():
+                    w_copy(c, way, 0, up).start()
+
+                @pl.when(go_left[way])
+                def _():
+                    w_copy(c, way, 1, down).start()
+
+            @pl.when(node != across)
             def _():
-                w_copy(c, w_right, up).wait_recv()
-
-            @pl.when(go_right)
-            def _():
-                w_copy(c, w_right, up).start()
-
-            @pl.when(go_left)
-            def _():
-                w_copy(c, w_left, down).start()
+                hop_copy(c).start()
 
         return 0
 
@@ -276,6 +298,16 @@
         return 0
 
     lax.fori_loop(0, rows_all // TB, aggregate, 0)
+
+    if relay:
+
+        @pl.when(node != feat)
+        def _():
+            def landed(c, _):
+                hop_copy(c).wait_recv()
+                return 0
+
+            lax.fori_loop(0, GC, landed, 0)
 
     def partial(g, c):
         rows = pl.ds(pl.multiple_of(g * R + c * RC, RC), RC)
@@ -392,13 +424,19 @@
     if relay:
 
         def drain(c, _):
-            @pl.when(go_right)
+            for way in range(2):
+
+                @pl.when(go_right[way])
+                def _():
+                    w_copy(c, way, 0, up).wait_send()
+
+                @pl.when(go_left[way])
+                def _():
+                    w_copy(c, way, 1, down).wait_send()
+
+            @pl.when(node != across)
             def _():
-                w_copy(c, w_right, up).wait_send()
-
-            @pl.when(go_left)
-            def _():
-                w_copy(c, w_left, down).wait_send()
+                hop_copy(c).wait_send()
 
             return 0
 
@@ -472,6 +510,7 @@
         out_specs=(VMEM, VMEM, ANY),
         scratch_shapes=[
             pltpu.VMEM((2, cw, H), BF16),
+            pltpu.VMEM((cw, H), BF16),
             pltpu.VMEM((capacity + 1, TB, TB), F32),
             pltpu.VMEM((rows_all, slot_rows), BF16),
             pltpu.VMEM((slot_rows, rows_all), BF16),
@@ -489,7 +528,8 @@
             [pltpu.VMEM((h, C, R // C, H), F32) for h in halves],
             dma((N,)),
             dma((N,)),
-            dma((2 * WC,)),
+            dma((2, 2, 2 * WC)),
+            dma((2, 2 * WC)),
             dma((2 * WC,)),
             dma((2 * WC,)),
             dma((F * C,)),

time: 102 us -> 185 us (1.81); the launches traced: 101 us -> 182 us
  Pallas kernels: 99.9 us -> 180 us
    pallas_call x1, Pallas kernels: 90.6 us -> 171 us  [on_device(): pl.pallas_call(functools.partial(main_kernel, (N, F, C, relay, WC)), out_...]
where the time goes in v3:
time: 185 us; the launch traced here: 182 us
  Pallas kernels  180 us (97%)
    pallas_call x1, Pallas kernels, on_device(): pl.pallas_call(functools.partial(main_kernel, (N, F, C, relay, WC)), out_...  171 us
    pallas_call x1, Pallas kernels, on_device(): pl.pallas_call(final_kernel, grid=(steps,), out_shape=(jax.ShapeDtypeStru...  6.52 us

profile of v3, /device:TPU:1, one launch (start us, length us, event | category | flops | bytes accessed | tf_op | source)
XLA Modules:
  0.0 181.7 jit_solution(16278625822920634459)
XLA Ops:
  1.3 2.8 %plan.1 = (f32[64,256]{1,0:T(8,128)}, f32[64,256]{1,0:T(8,128)}, s32[1,128]{1,0:T(1,128)}, bf16[1024,256]{1,0:T(8,128)(2,1)}) custom-call(s32[1]{0:T(128)S(6)} %copy.12.counts, s32[2,4]{1,0:T(2,128)} %bitcast.10, s32[3,1,64]{2,1,0:T(1,128)} %bitcast.12, s32[64,256]{1,0:T(8,128)} %bitcast.7, bf16[4096,256]{1,0:T(8,128)(2,1)} %features.3), custom_call_target="tpu_custom_call" | custom-call | tf_op jit(solution)/shard_map/plan/pallas_call | solution.py:476
  4.1 171.0 %layer.1 = (bf16[256,1024]{1,0:T(8,128)(2,1)}, bf16[1024,256]{1,0:T(8,128)(2,1)}, bf16[4096,256]{1,0:T(8,128)(2,1)}) custom-call(bf16[1024,256]{1,0:T(8,128)(2,1)} %get-tuple-element.11.out_blocks, bf16[256,1024]{1,0:T(8,128)(2,1)} %w_self.1, bf16[256,1024]{1,0:T(8,128)(2,1)} %w_neigh.1, f32[1,1024]{1,0:T(1,128)} %bitcast.8, ...), custom_call_target="tpu_custom_call" | custom-call | tf_op jit(solution)/shard_map/layer/pallas_call | solution.py:502
  175.2 6.5 %finish.1 = (bf16[4096,256]{1,0:T(8,128)(2,1)}, bf16[256,1024]{1,0:T(8,128)(2,1)}) custom-call(s32[2,4]{1,0:T(2,128)} %bitcast.11, bf16[4096,256]{1,0:T(8,128)(2,1)} %get-tuple-element.15.base, bf16[1024,256]{1,0:T(8,128)(2,1)} %get-tuple-element.16.back, bf16[256,1024]{1,0:T(8,128)(2,1)} %get-tuple-element.17.layer), custom_call_target="tpu_custom_call" | custom-call | tf_op jit(solution)/shard_map/finish/pallas_call | solution.py:560

commit v4 on v3

--- a/solution.py
+++ b/solution.py
@@ -203,6 +203,15 @@
     go_right = [(node >= r) & (node < N - 1) for r in roots]
     go_left = [(node <= r) & (node > 0) for r in roots]
 
+    def pass_on(c, way, here):
+        @pl.when(here & go_right[way])
+        def _():
+            w_copy(c, way, 0, up).start()
+
+        @pl.when(here & go_left[way])
+        def _():
+            w_copy(c, way, 1, down).start()
+
     if relay:
 
         @pl.when(node == feat)
@@ -213,6 +222,12 @@
         @pl.when(node == across)
         def _():
             wvia[...] = w_neigh[...]
+        def launch(c, _):
+            for way in range(2):
+                pass_on(c, way, node == roots[way])
+            return 0
+
+        lax.fori_loop(0, GC, launch, 0)
     else:
         wbuf[0] = w_self[...]
         wbuf[1] = w_neigh[...]
@@ -257,13 +272,7 @@
                 def _():
                     w_copy(c, way, 0, up).wait_recv()
 
-                @pl.when(go_right[way])
-                def _():
-                    w_copy(c, way, 0, up).start()
-
-                @pl.when(go_left[way])
-                def _():
-                    w_copy(c, way, 1, down).start()
+                pass_on(c, way, node != roots[way])
 
             @pl.when(node != across)
             def _():
@@ -556,7 +565,7 @@
         dst_ids.reshape(1, -1),
         cotangent,
     )
-    steps = math.gcd(math.gcd(feat_rows // TB, R // 16), 8)
+    steps = math.gcd(math.gcd(feat_rows // TB, R // 16), 2)
     grad_rows, layer_out = pl.pallas_call(
         final_kernel,
         grid=(steps,),

time: 185 us -> 86.8 us (0.47); the launches traced: 182 us -> 86 us
  Pallas kernels: 180 us -> 84.7 us
    pallas_call x1, Pallas kernels: 171 us -> 78.6 us  [on_device(): pl.pallas_call(functools.partial(main_kernel, (N, F, C, relay, WC)), out_...]
    pallas_call x1, Pallas kernels: 6.52 us -> 3.24 us  [on_device(): pl.pallas_call(final_kernel, grid=(steps,), out_shape=(jax.ShapeDtypeStru...]
where the time goes in v4:
time: 86.8 us; the launch traced here: 86 us
  Pallas kernels  84.7 us (98%)
  between operations  1.29 us (1%)
    pallas_call x1, Pallas kernels, on_device(): pl.pallas_call(functools.partial(main_kernel, (N, F, C, relay, WC)), out_...  78.6 us
    pallas_call x1, Pallas kernels, on_device(): pl.pallas_call(final_kernel, grid=(steps,), out_shape=(jax.ShapeDtypeStru...  3.24 us
    pallas_call x1, Pallas kernels, on_device(): pl.pallas_call(functools.partial(plan_kernel, slots), out_shape=(jax.Shap...  2.84 us

profile of v4, /device:TPU:1, one launch (start us, length us, event | category | flops | bytes accessed | tf_op | source)
XLA Modules:
  0.0 86.0 jit_solution(12262152477839625273)
XLA Ops:
  1.3 2.8 %plan.1 = (f32[64,256]{1,0:T(8,128)}, f32[64,256]{1,0:T(8,128)}, s32[1,128]{1,0:T(1,128)}, bf16[1024,256]{1,0:T(8,128)(2,1)}) custom-call(s32[1]{0:T(128)S(6)} %copy.12.counts, s32[2,4]{1,0:T(2,128)} %bitcast.10, s32[3,1,64]{2,1,0:T(1,128)} %bitcast.12, s32[64,256]{1,0:T(8,128)} %bitcast.7, bf16[4096,256]{1,0:T(8,128)(2,1)} %features.3), custom_call_target="tpu_custom_call" | custom-call | tf_op jit(solution)/shard_map/plan/pallas_call | solution.py:485
  4.1 78.6 %layer.1 = (bf16[256,1024]{1,0:T(8,128)(2,1)}, bf16[1024,256]{1,0:T(8,128)(2,1)}, bf16[4096,256]{1,0:T(8,128)(2,1)}) custom-call(bf16[1024,256]{1,0:T(8,128)(2,1)} %get-tuple-element.11.out_blocks, bf16[256,1024]{1,0:T(8,128)(2,1)} %w_self.1, bf16[256,1024]{1,0:T(8,128)(2,1)} %w_neigh.1, f32[1,1024]{1,0:T(1,128)} %bitcast.8, ...), custom_call_target="tpu_custom_call" | custom-call | tf_op jit(solution)/shard_map/layer/pallas_call | solution.py:511
  82.7 3.2 %finish.1 = (bf16[4096,256]{1,0:T(8,128)(2,1)}, bf16[256,1024]{1,0:T(8,128)(2,1)}) custom-call(s32[2,4]{1,0:T(2,128)} %bitcast.11, bf16[4096,256]{1,0:T(8,128)(2,1)} %get-tuple-element.15.base, bf16[1024,256]{1,0:T(8,128)(2,1)} %get-tuple-element.16.back, bf16[256,1024]{1,0:T(8,128)(2,1)} %get-tuple-element.17.layer), custom_call_target="tpu_custom_call" | custom-call | tf_op jit(solution)/shard_map/finish/pallas_call | solution.py:569

commit v5 on v4

--- a/solution.py
+++ b/solution.py
@@ -243,6 +243,19 @@
     lane_id = lax.broadcasted_iota(jnp.int32, (TB, TB), 1)
     prefix[0] = jnp.zeros((TB, TB), F32)
 
+    def relay_piece(c):
+        for way in range(2):
+
+            @pl.when(node != roots[way])
+            def _():
+                w_copy(c, way, 0, up).wait_recv()
+
+            pass_on(c, way, node != roots[way])
+
+        @pl.when(node != across)
+        def _():
+            hop_copy(c).start()
+
     def load(c, _):
         running = prefix[c * group]
         for k in range(group):
@@ -266,17 +279,9 @@
             own[rows, :] = dot_nn(hot, features[...]).astype(BF16)
         if relay:
 
-            for way in range(2):
-
-                @pl.when(node != roots[way])
-                def _():
-                    w_copy(c, way, 0, up).wait_recv()
-
-                pass_on(c, way, node != roots[way])
-
-            @pl.when(node != across)
+            @pl.when(c >= WC)
             def _():
-                hop_copy(c).start()
+                relay_piece(c - WC)
 
         return 0
 
@@ -296,6 +301,8 @@
         return 0
 
     lax.fori_loop(0, n_dst, assemble, 0)
+    if relay:
+        relay_piece(WC)
 
     for d in range(1, N):
         exchange(out_blocks, recv, f_send, f_recv, d).wait_recv()
@@ -307,6 +314,13 @@
         return 0
 
     lax.fori_loop(0, rows_all // TB, aggregate, 0)
+    if relay:
+
+        def rest(c, _):
+            relay_piece(c)
+            return 0
+
+        lax.fori_loop(WC + 1, GC, rest, 0)
 
     if relay:
 

time: 86.8 us -> 87.3 us (level)
  no operation moved by 1% of the time
where the time goes in v5:
time: 87.3 us; the launch traced here: 86.2 us
  Pallas kernels  84.9 us (97%)
  between operations  1.29 us (1%)
    pallas_call x1, Pallas kernels, on_device(): pl.pallas_call(functools.partial(main_kernel, (N, F, C, relay, WC)), out_...  78.8 us
    pallas_call x1, Pallas kernels, on_device(): pl.pallas_call(final_kernel, grid=(steps,), out_shape=(jax.ShapeDtypeStru...  3.23 us
    pallas_call x1, Pallas kernels, on_device(): pl.pallas_call(functools.partial(plan_kernel, slots), out_shape=(jax.Shap...  2.84 us

profile of v5, /device:TPU:1, one launch (start us, length us, event | category | flops | bytes accessed | tf_op | source)
XLA Modules:
  0.0 86.2 jit_solution(1807869487951388974)
XLA Ops:
  1.3 2.8 %plan.1 = (f32[64,256]{1,0:T(8,128)}, f32[64,256]{1,0:T(8,128)}, s32[1,128]{1,0:T(1,128)}, bf16[1024,256]{1,0:T(8,128)(2,1)}) custom-call(s32[1]{0:T(128)S(6)} %copy.12.counts, s32[2,4]{1,0:T(2,128)} %bitcast.10, s32[3,1,64]{2,1,0:T(1,128)} %bitcast.12, s32[64,256]{1,0:T(8,128)} %bitcast.7, bf16[4096,256]{1,0:T(8,128)(2,1)} %features.3), custom_call_target="tpu_custom_call" | custom-call | tf_op jit(solution)/shard_map/plan/pallas_call | solution.py:499
  4.1 78.8 %layer.1 = (bf16[256,1024]{1,0:T(8,128)(2,1)}, bf16[1024,256]{1,0:T(8,128)(2,1)}, bf16[4096,256]{1,0:T(8,128)(2,1)}) custom-call(bf16[1024,256]{1,0:T(8,128)(2,1)} %get-tuple-element.11.out_blocks, bf16[256,1024]{1,0:T(8,128)(2,1)} %w_self.1, bf16[256,1024]{1,0:T(8,128)(2,1)} %w_neigh.1, f32[1,1024]{1,0:T(1,128)} %bitcast.8, ...), custom_call_target="tpu_custom_call" | custom-call | tf_op jit(solution)/shard_map/layer/pallas_call | solution.py:525
  82.9 3.2 %finish.1 = (bf16[4096,256]{1,0:T(8,128)(2,1)}, bf16[256,1024]{1,0:T(8,128)(2,1)}) custom-call(s32[2,4]{1,0:T(2,128)} %bitcast.11, bf16[4096,256]{1,0:T(8,128)(2,1)} %get-tuple-element.15.base, bf16[1024,256]{1,0:T(8,128)(2,1)} %get-tuple-element.16.back, bf16[256,1024]{1,0:T(8,128)(2,1)} %get-tuple-element.17.layer), custom_call_target="tpu_custom_call" | custom-call | tf_op jit(solution)/shard_map/finish/pallas_call | solution.py:583
